TPU v7x, 32 devices: a whole 2x2x4 slice. The times are simulated.
32 devices in a mesh: shard: 8 (over y, x, core), tensor: 4 (over z).
Axes of the slice: x: 2, y: 2, z: 4, core: 2. Of those that a mesh axis runs over, the one named last changes fastest.
Arguments:
- grads: bfloat16 [4096, 2048], P('shard', 'tensor'), may hold values from -120 to 120
- assignment: int32 [4, 8], P('tensor'), may hold values from 0 to 7, as said below
- moment: float32 [8, 2048, 512], P('shard', 'tensor'), may hold values from -6 to 6
- second: float32 [8, 2048, 512], P('shard', 'tensor'), may hold values from 0.2 to 2
- left_stats: float32 [8, 2048, 512], P('shard', 'tensor'), may hold values from -0.02 to 3.1, as said below
- right_stats: float32 [8, 2048, 512], P('shard', 'tensor'), may hold values from -0.02 to 3.1, as said below
- left_basis: float32 [8, 2048, 512], P('shard', 'tensor'), may hold values from -0.25 to 0.25
- right_basis: float32 [8, 2048, 512], P('shard', 'tensor'), may hold values from -0.25 to 0.25
Outputs:
- update: bfloat16 [4096, 2048], P('shard', 'tensor')
- new_moment: float32 [8, 2048, 512], P('shard', 'tensor')
- new_second: float32 [8, 2048, 512], P('shard', 'tensor')
- new_left_stats: float32 [8, 2048, 512], P('shard', 'tensor')
- new_right_stats: float32 [8, 2048, 512], P('shard', 'tensor')
- new_left_basis: float32 [8, 2048, 512], P('shard', 'tensor')
- new_right_basis: float32 [8, 2048, 512], P('shard', 'tensor')
Inputs may be any that keep to these rules, and one draw needn't show every extreme that they name: `assignment`: within each block column the slots are distinct; slot a lies on index a // 1 of shard as its slot a % 1; in every block column some index of shard holds 1 block. `left_stats`: statistics carried from earlier steps. `right_stats`: statistics carried from earlier steps.
All inputs are finite; a program needn't handle non-finite values.
Results may differ from a plain program's by a relative error of at most 0.0004.
Values may be sent and summed in bfloat16 or wider, within the bound.
A program may use at most 128 MiB of HBM per device.

v0:
```python
import jax
import jax.numpy as jnp
from jax import lax
from jax.sharding import PartitionSpec as P

NS_ITERS = 2


BETA_MOMENT = 0.9
BETA_SECOND = 0.9
BETA_STATS = 0.9
ADAM_EPSILON = 1e-08
CLIP_RMS = 1.0
QUINTIC_A = 3.4445
QUINTIC_B = -4.775
QUINTIC_C = 2.0315


def highest_dot(left_side, right_side):
    return jnp.dot(
        left_side, right_side, precision=lax.Precision.HIGHEST, preferred_element_type=jnp.float32
    )


def orthonormal(product):
    iterate = product * lax.rsqrt(jnp.sum(product * product) + 1e-12)
    for sweep in range(NS_ITERS):
        gram_matrix = highest_dot(iterate.T, iterate)
        polynomial = QUINTIC_B * gram_matrix + QUINTIC_C * highest_dot(gram_matrix, gram_matrix)
        iterate = QUINTIC_A * iterate + highest_dot(iterate, polynomial)
    return iterate


def tile_update(grad_tile, factor, moment, second, left_old, right_old, left_rot, right_rot):
    block_size = grad_tile.shape[0]
    grad_float = grad_tile.astype(jnp.float32) * factor
    scale_stats = (1.0 - BETA_STATS) * factor * factor / block_size
    left_new = BETA_STATS * left_old + scale_stats * jnp.dot(
        grad_tile, grad_tile.T, preferred_element_type=jnp.float32
    )
    right_new = BETA_STATS * right_old + scale_stats * jnp.dot(
        grad_tile.T, grad_tile, preferred_element_type=jnp.float32
    )
    moment_new = BETA_MOMENT * moment + (1.0 - BETA_MOMENT) * grad_float
    rotated = highest_dot(highest_dot(left_rot.T, grad_float), right_rot)
    rotated_moment = highest_dot(highest_dot(left_rot.T, moment_new), right_rot)
    second_new = BETA_SECOND * second + (1.0 - BETA_SECOND) * rotated * rotated
    direction = rotated_moment / (jnp.sqrt(second_new) + ADAM_EPSILON)
    update = highest_dot(highest_dot(left_rot, direction), right_rot.T).astype(jnp.bfloat16)
    left_basis_new = orthonormal(highest_dot(left_old, left_rot))
    right_basis_new = orthonormal(highest_dot(right_old, right_rot))
    return (update, moment_new, second_new, left_new, right_new, left_basis_new, right_basis_new)


def shards(grads, assignment, moment, second, left_stats, right_stats, left_basis, right_basis):
    shard_count = lax.axis_size("shard")
    my_shard = lax.axis_index("shard")
    block_size = grads.shape[1]
    slot_count = moment.shape[0]
    entries = grads.shape[0] * grads.shape[1] * shard_count * lax.axis_size("tensor")
    grad_float = grads.astype(jnp.float32)
    energy = lax.psum(jnp.sum(grad_float * grad_float), ("shard", "tensor"))
    factor = jnp.minimum(1.0, CLIP_RMS / jnp.sqrt(energy / entries + 1e-12))
    slot_table = assignment[0]
    tile_ids = jnp.arange(shard_count, dtype=jnp.int32)
    slot_index = 0
    matches = slot_table == my_shard * slot_count + slot_index
    in_use = [jnp.any(matches)]
    tile_of = [jnp.sum(jnp.where(matches, tile_ids, 0))]
    empty_tiles = jnp.zeros((slot_count, block_size, block_size), jnp.bfloat16)
    tiles_carry = empty_tiles
    shard_rows = lax.all_gather(grads, "shard", axis=0, tiled=True)
    row_index = jnp.arange(shard_rows.shape[0], dtype=jnp.int32)
    slot_index = 0
    tile_row = row_index - tile_of[slot_index] * block_size
    inside = in_use[slot_index] & (tile_row >= 0) & (tile_row < block_size)
    tile_row = jnp.where(inside, tile_row, block_size)
    tiles_carry = tiles_carry.at[slot_index, tile_row].set(shard_rows, mode="drop")
    slot_index = 0
    operands = (
        tiles_carry[slot_index],
        moment[slot_index],
        second[slot_index],
        left_stats[slot_index],
        right_stats[slot_index],
        left_basis[slot_index],
        right_basis[slot_index],
    )
    outcome = lax.cond(
        in_use[slot_index],
        lambda values: tile_update(values[0], factor, *values[1:]),
        lambda values: (jnp.zeros_like(values[0]),) + tuple(values[1:]),
        operands,
    )
    results = [outcome]
    updates = jnp.stack([outcome[0] for outcome in results])
    new_states = tuple(
        (jnp.stack([outcome[member] for outcome in results]) for member in range(1, 7))
    )
    row_index = jnp.arange(block_size * lax.axis_size("shard"), dtype=jnp.int32)
    slot_index = 0
    tile_row = row_index - tile_of[slot_index] * block_size
    inside = in_use[slot_index] & (tile_row >= 0) & (tile_row < block_size)
    taken = jnp.take(updates[slot_index], jnp.clip(tile_row, 0, block_size - 1), axis=0).astype(
        jnp.float32
    )
    partial_value = jnp.where(inside[:, None], taken, 0.0)
    update_out = lax.psum_scatter(
        partial_value.astype(jnp.bfloat16), "shard", scatter_dimension=0, tiled=True
    )
    return (update_out,) + new_states


def solution(mesh):
    placed = (
        P("shard", "tensor"),
        P("tensor", None),
        P("shard", "tensor", None),
        P("shard", "tensor", None),
        P("shard", "tensor", None),
        P("shard", "tensor", None),
        P("shard", "tensor", None),
        P("shard", "tensor", None),
    )
    return jax.shard_map(
        shards,
        mesh=mesh,
        in_specs=placed,
        out_specs=(
            P("shard", "tensor"),
            P("shard", "tensor", None),
            P("shard", "tensor", None),
            P("shard", "tensor", None),
            P("shard", "tensor", None),
            P("shard", "tensor", None),
            P("shard", "tensor", None),
        ),
        check_vma=False,
    )
```

profile of v0, /device:TPU:0, one launch (start us, length us, event | category | flops | bytes accessed | tf_op | source)
XLA Modules:
  0.0 223.5 jit_solution(16228758280795699595)
XLA Ops:
  7.2 0.0 all-gather.2.cloned.1.call-start
  7.2 2.4 %copy.35 = f32[1,512,512]{2,1,0:T(8,128)} copy(f32[1,512,512]{2,1,0:T(8,128)} %param.12) | data formatting | bytes 2097152
  9.6 2.3 %copy.36 = f32[1,512,512]{2,1,0:T(8,128)} copy(f32[1,512,512]{2,1,0:T(8,128)} %param.13) | data formatting | bytes 2097152
  11.9 1.0 copy.37
  12.9 0.0 copy-start.1
  12.9 1.0 copy.38
  13.9 0.0 all-gather.2.cloned.1.call-update
  13.9 0.0 reduce-scatter.2.cloned.1.call-start
  14.0 0.9 multiply_reduce_fusion.2
  14.8 42.3 %psum.7 = f32[]{:T(128)} all-reduce(f32[]{:T(128)} %multiply_reduce_fusion.2), channel_id=1, replica_groups=mesh['shard'=8,'tensor'=4] {'shard','tensor'}, use_global_device_ids=true, to_apply=%region_4.5 | all-reduce | flops 1 | bytes 8 | tf_op jit(solution)/shard_map/psum | solution.py:62
  57.2 0.6 compare_reduce_fusion
  58.4 0.6 fusion.32
  59.7 0.7 fusion.29
  60.4 0.7 compare_select_fusion
  61.2 0.1 fusion.24
  61.3 0.1 and_reduce_fusion
  61.4 0.0 all-gather.2.cloned.1.call-done
  61.5 18.6 %scatter_custom_fusion = bf16[512,512]{1,0:T(8,128)(2,1)S(1)} fusion(s32[4096]{0:T(1024)S(1)} %broadcast_select_fusion, bf16[4096,512]{1,0:T(8,128)(2,1)} %all-gather.2.cloned.1.call-done, bf16[]{:T(256)} %constant.74.clone.1), kind=kCustom, calls=%fused_computation.43 | custom fusion | bytes 524800
  80.1 62.0 %conditional.1 = (bf16[512,512]{1,0:T(8,128)(2,1)S(1)}, f32[512,512]{1,0:T(8,128)}, f32[512,512]{1,0:T(8,128)}, f32[512,512]{1,0:T(8,128)}, f32[512,512]{1,0:T(8...) conditional(s32[]{:T(128)} %convert_element_type.20, (f32[512,512]{1,0:T(8,128)}, f32[512,512]{1,0:T(8,128)}, ...), branch_computations={%region_5.6_spmd, %region_6.9_spmd} | conditional | flops 32762232832 | bytes 101188040 | solution.py:89
  80.3 4.6 %multiply_reduce_fusion.1 = (f32[]{:T(128)}, f32[512,512]{1,0:T(8,128)}) fusion(f32[512,512]{1,0:T(8,128)} %get-tuple-element.64, f32[512,512]{1,0:T(8,128)S(1)} %get-tuple-element.61), kind=kOutput, calls=%fused_computation.23 | convolution fusion | flops 1611137024 | bytes 3145732 | tf_op jit(solution)/shard_map/cond/branch_1_fun/dot_general | solution.py:20
  85.6 3.5 %fusion.11 = f32[512,512]{1,0:T(8,128)S(1)} fusion(f32[512,512]{1,0:T(8,128)} %get-tuple-element.88, f32[]{:T(128)S(6)} %rsqrt.9), kind=kOutput, calls=%fused_computation.30 | convolution fusion | flops 1610874880 | bytes 2097156 | tf_op jit(solution)/shard_map/cond/branch_1_fun/dot_general | solution.py:20
  89.2 1.9 fusion.3
  91.1 1.9 convolution_add_fusion.3
  92.9 1.9 fusion.35
  94.8 1.9 fusion.2
  96.7 3.0 %convolution_add_fusion.2 = f32[512,512]{1,0:T(8,128)} fusion(f32[512,512]{1,0:T(8,128)S(1)} %convolution_add_fusion.3, f32[512,512]{1,0:T(8,128)S(1)} %fusion.2), kind=kOutput, calls=%fused_computation.9 | convolution fusion | flops 1611137024 | bytes 3145728 | tf_op jit(solution)/shard_map/cond/branch_1_fun/dot_general | solution.py:20
  100.4 1.9 fusion.7
  102.3 4.1 %fusion.6 = f32[512,512]{1,0:T(8,128)} fusion(f32[512,512]{1,0:T(8,128)} %get-tuple-element.63, f32[512,512]{1,0:T(8,128)S(1)} %fusion.7, f32[512,512]{1,0:T(8,128)S(1)} %get-tuple-element.62), kind=kOutput, calls=%fused_computation.21 | convolution fusion | flops 1611661312 | bytes 4194304 | tf_op jit(solution)/shard_map/cond/branch_1_fun/dot_general | solution.py:20
  106.4 0.6 multiply_add_fusion
  106.9 1.9 fusion.33
  108.8 2.0 convolution_divide_fusion
  110.9 4.4 %fusion.34 = f32[512,512]{1,0:T(8,128)} fusion(f32[512,512]{1,0:T(8,128)S(1)} %convolution_divide_fusion, f32[512,512]{1,0:T(8,128)S(1)} %get-tuple-element.61), kind=kOutput, calls=%fused_computation.67 | convolution fusion | flops 1610612736 | bytes 3145728 | tf_op jit(solution)/shard_map/cond/branch_1_fun/dot_general | solution.py:20
  115.3 0.1 copy.27
  115.4 3.8 %multiply_reduce_fusion = (f32[]{:T(128)}, f32[512,512]{1,0:T(8,128)}) fusion(f32[512,512]{1,0:T(8,128)S(1)} %copy-done.8, f32[512,512]{1,0:T(8,128)S(1)} %get-tuple-element.62), kind=kOutput, calls=%fused_computation.22 | convolution fusion | flops 1611137024 | bytes 3145732 | tf_op jit(solution)/shard_map/cond/branch_1_fun/dot_general | solution.py:20
  119.9 3.5 %fusion.8 = f32[512,512]{1,0:T(8,128)S(1)} fusion(f32[512,512]{1,0:T(8,128)} %get-tuple-element.90, f32[]{:T(128)S(6)} %rsqrt.10), kind=kOutput, calls=%fused_computation.27 | convolution fusion | flops 1610874880 | bytes 2097156 | tf_op jit(solution)/shard_map/cond/branch_1_fun/dot_general | solution.py:20
  123.5 1.9 fusion.1
  125.4 1.9 convolution_add_fusion.1
  127.3 1.9 fusion.36
  129.1 1.9 fusion
  131.0 2.0 convolution_add_fusion
  133.1 3.5 %convolution_convert_fusion = bf16[512,512]{1,0:T(8,128)(2,1)S(1)} fusion(f32[512,512]{1,0:T(8,128)S(1)} %copy-done.9, f32[512,512]{1,0:T(8,128)S(1)} %get-tuple-element.62), kind=kOutput, calls=%fused_computation.20 | convolution fusion | flops 1610874880 | bytes 2621440 | tf_op jit(solution)/shard_map/cond/branch_1_fun/dot_general | solution.py:20
  136.5 0.1 copy.28
  136.6 2.7 %fusion.5 = f32[512,512]{1,0:T(8,128)} fusion(f32[512,512]{1,0:T(8,128)} %get-tuple-element.64, bf16[1,512,512]{2,1,0:T(8,128)(2,1)S(1)} %get-tuple-element.59, f32[]{:T(128)S(6)} %div.10), kind=kOutput, calls=%fused_computation.18 | convolution fusion | flops 269221888 | bytes 2621444 | tf_op jit(solution)/shard_map/cond/branch_1_fun/dot_general | solution.py:38
  139.3 2.7 %fusion.4 = f32[512,512]{1,0:T(8,128)} fusion(f32[512,512]{1,0:T(8,128)} %get-tuple-element.65, bf16[1,512,512]{2,1,0:T(8,128)(2,1)S(1)} %get-tuple-element.59, f32[]{:T(128)S(6)} %div.10), kind=kOutput, calls=%fused_computation.16 | convolution fusion | flops 269221888 | bytes 2621444 | tf_op jit(solution)/shard_map/cond/branch_1_fun/dot_general | solution.py:41
  142.2 17.4 %gather_fusion = bf16[4096,512]{1,0:T(8,128)(2,1)} fusion(bf16[512,512]{1,0:T(8,128)(2,1)S(1)} %get-tuple-element.80, s32[4096]{0:T(1024)S(1)} %broadcast_clamp_fusion), kind=kCustom, calls=%fused_computation | custom fusion | bytes 8404992 | tf_op jit(solution)/shard_map/jit(_take)/gather | solution.py:104
  159.5 5.2 %select_convert_fusion = bf16[4096,512]{1,0:T(8,128)(2,1)} fusion(bf16[4096,512]{1,0:T(8,128)(2,1)} %gather_fusion, pred[4096]{0:T(1024)(128)(4,1)S(1)} %get-tuple-element.93, pred[4096]{0:T(1024)(128)(4,1)S(1)} %get-tuple-element.94), kind=kLoop, calls=%fused_computation.41 | loop fusion | flops 8388608 | bytes 8396800 | tf_op jit(solution)/shard_map/convert_element_type | solution.py:109
  164.8 0.0 reduce-scatter.2.cloned.1.call-update
  164.8 51.6 %reduce-scatter.2.cloned.1.call-done = bf16[512,512]{1,0:T(8,128)(2,1)} async-done(((bf16[4096,512]{1,0:T(8,128)(2,1)}), bf16[512,512]{1,0:T(8,128)(2,1)}) %reduce-scatter.2.cloned.1.call-update) | async-done | bytes 524304 | tf_op jit(solution)/shard_map/reduce_scatter | solution.py:108
  (37 shorter events, 0.1 us)
Async XLA Ops:
  7.2 4.7 %copy-start.13 = (f32[1,512,512]{2,1,0:T(8,128)S(1)}, f32[1,512,512]{2,1,0:T(8,128)}, u32[]{:S(2)}) copy-start(f32[1,512,512]{2,1,0:T(8,128)} %param.14) | copy-start | bytes 3145732
  7.2 54.3 %all-gather.2.cloned.1.call-start = ((), (), s32[]{:S(2)}) async-start(), calls=%async_computation.1 | async-start | bytes 4718592 | tf_op jit(solution)/shard_map/all_gather | solution.py:72
  7.2 5.7 %copy-start.14 = (f32[1,512,512]{2,1,0:T(8,128)S(1)}, f32[1,512,512]{2,1,0:T(8,128)}, u32[]{:S(2)}) copy-start(f32[1,512,512]{2,1,0:T(8,128)} %param.15) | copy-start | bytes 3145732
  11.9 2.1 copy-start.12
  12.9 44.3 %copy-start.17 = (s32[1,8]{1,0:T(1,128)S(1)}, s32[1,8]{1,0:T(1,128)}, u32[]{:S(2)}) copy-start(s32[1,8]{1,0:T(1,128)} %param.11) | copy-start | bytes 100
  12.9 48.3 %copy-start.15 = (s32[2]{0:T(128)S(1)}, s32[2]{0:T(128)}, u32[]{:S(2)}) copy-start(s32[2]{0:T(128)} %constant.86) | copy-start | bytes 28
  12.9 48.4 %copy-start.16 = (s32[2]{0:T(128)S(1)}, s32[2]{0:T(128)}, u32[]{:S(2)}) copy-start(s32[2]{0:T(128)} %constant.89) | copy-start | bytes 28
  12.9 67.2 %copy-start.1 = (f32[1,512,512]{2,1,0:T(8,128)S(1)}, f32[1,512,512]{2,1,0:T(8,128)}, u32[]{:S(2)}) copy-start(f32[1,512,512]{2,1,0:T(8,128)} %param.16) | copy-start | bytes 3145732
  12.9 67.2 %copy-start.3 = (f32[1,512,512]{2,1,0:T(8,128)S(1)}, f32[1,512,512]{2,1,0:T(8,128)}, u32[]{:S(2)}) copy-start(f32[1,512,512]{2,1,0:T(8,128)} %param.17) | copy-start | bytes 3145732
  13.9 202.5 %reduce-scatter.2.cloned.1.call-start = ((), (), s32[]{:S(2)}) async-start(), calls=%async_computation.2 | async-start | bytes 4718592 | tf_op jit(solution)/shard_map/reduce_scatter | solution.py:108
  85.6 5.4 %copy-start.7 = (f32[512,512]{1,0:T(8,128)S(1)}, f32[512,512]{1,0:T(8,128)}, u32[]{:S(2)}) copy-start(f32[512,512]{1,0:T(8,128)} %get-tuple-element.88) | copy-start | bytes 3145732 | tf_op jit(solution)/shard_map/cond
  100.4 6.0 %copy-start.4 = (f32[512,512]{1,0:T(8,128)S(1)}, f32[512,512]{1,0:T(8,128)}, u32[]{:S(2)}) copy-start(f32[512,512]{1,0:T(8,128)} %get-tuple-element.58) | copy-start | bytes 3145732 | tf_op jit(solution)/shard_map/cond
  106.3 2.5 %copy-start.11 = (f32[512,512]{1,0:T(8,128)S(1)}, f32[512,512]{1,0:T(8,128)}, u32[]{:S(2)}) copy-start(f32[512,512]{1,0:T(8,128)} %fusion.6) | copy-start | bytes 3145732 | tf_op jit(solution)/shard_map/cond
  106.9 8.4 %copy-start.5 = (f32[512,512]{1,0:T(8,128)}, f32[512,512]{1,0:T(8,128)S(1)}, u32[]{:S(2)}) copy-start(f32[512,512]{1,0:T(8,128)S(1)} %multiply_add_fusion) | copy-start | bytes 3145732 | tf_op jit(solution)/shard_map/cond
  108.8 6.5 %copy-start.10 = (f32[512,512]{1,0:T(8,128)S(1)}, f32[512,512]{1,0:T(8,128)}, u32[]{:S(2)}) copy-start(f32[512,512]{1,0:T(8,128)} %convolution_add_fusion.2) | copy-start | bytes 3145732 | tf_op jit(solution)/shard_map/cond
  108.8 6.6 %copy-start.8 = (f32[512,512]{1,0:T(8,128)S(1)}, f32[512,512]{1,0:T(8,128)}, u32[]{:S(2)}) copy-start(f32[512,512]{1,0:T(8,128)} %get-tuple-element.65) | copy-start | bytes 3145732 | tf_op jit(solution)/shard_map/cond
  119.9 5.4 %copy-start.6 = (f32[512,512]{1,0:T(8,128)S(1)}, f32[512,512]{1,0:T(8,128)}, u32[]{:S(2)}) copy-start(f32[512,512]{1,0:T(8,128)} %get-tuple-element.90) | copy-start | bytes 3145732 | tf_op jit(solution)/shard_map/cond
  127.3 5.8 %copy-start.9 = (f32[512,512]{1,0:T(8,128)S(1)}, f32[512,512]{1,0:T(8,128)}, u32[]{:S(2)}) copy-start(f32[512,512]{1,0:T(8,128)} %fusion.34) | copy-start | bytes 3145732 | tf_op jit(solution)/shard_map/cond
  142.2 17.4 %copy-start = (f32[512,512]{1,0:T(8,128)}, f32[512,512]{1,0:T(8,128)S(1)}, u32[]{:S(2)}) copy-start(f32[512,512]{1,0:T(8,128)S(1)} %get-tuple-element.85) | copy-start | bytes 3145732
  142.2 17.4 %copy-start.2 = (f32[512,512]{1,0:T(8,128)}, f32[512,512]{1,0:T(8,128)S(1)}, u32[]{:S(2)}) copy-start(f32[512,512]{1,0:T(8,128)S(1)} %get-tuple-element.86) | copy-start | bytes 3145732
Sparse Core Ops, SparseCore 0:
  14.0 39.7 all-gather.1
  164.9 51.4 reduce-scatter.1
where the time goes:
time: 228 us; the launch traced here: 224 us
  matrix products  58.7 us (26%)
  waiting for transfers between devices  51.7 us (23%)
  local copies, waits for them, and re-layouts  42.8 us (19%)
  blocking collectives  42.3 us (19%)
  between operations  15.7 us (7%)
  other arithmetic  9.63 us (4%)
  loops' own time  2.61 us (1%)
    dot_general x20, matrix products, highest_dot(): jnp.dot(left_side, right_side, precision=lax.Precision.HIGHEST, preferred...  53.3 us
    reduce_scatter x1, waiting for transfers between devices, shards(): lax.psum_scatter(partial_value.astype(jnp.bfloat16), 'shard', scatter_dim...  51.6 us
    psum x1, blocking collectives, shards(): energy = lax.psum(jnp.sum(grad_float * grad_float), ('shard', 'tensor'))  42.3 us
    unnamed x25, local copies, waits for them, and re-layouts  25.3 us
    gather x1, local copies, waits for them, and re-layouts, shards(): jnp.take(updates[slot_index], jnp.clip(tile_row, 0, block_size - 1), axis=0)  17.4 us
    convert_element_type x1, other arithmetic, shards(): partial_value.astype(jnp.bfloat16)  5.25 us
  transfers between devices with their start and end apart: 2, of which 1 were waited for; matrix products, arithmetic and copies ran while one was open for 2% of the time, Pallas kernels for 0%

commit v1 on v0

v1 whole, which is shorter than its diff:
```python
import functools

import jax
import jax.numpy as jnp
from jax import lax
from jax.experimental import pallas as pl
from jax.experimental.pallas import tpu as pltpu
from jax.sharding import PartitionSpec as P

NS_ITERS = 2
BETA_MOMENT = 0.9
BETA_SECOND = 0.9
BETA_STATS = 0.9
ADAM_EPSILON = 1e-08
CLIP_RMS = 1.0
QUINTIC_A = 3.4445
QUINTIC_B = -4.775
QUINTIC_C = 2.0315
MESH = pl.DeviceIdType.MESH
F32 = jnp.float32
BF16 = jnp.bfloat16


def nn(a, b):
    return jnp.dot(a, b, preferred_element_type=F32)


def nt(a, b):
    return lax.dot_general(a, b, (((1,), (1,)), ((), ())), preferred_element_type=F32)


def split(x):
    high = x.astype(BF16)
    return high, (x - high.astype(F32)).astype(BF16)


def put(ref, x, order, axis):
    n = x.shape[0]
    parts = split(x)
    for place, part in enumerate(order):
        if axis:
            ref[:, place * n : (place + 1) * n] = parts[part]
        else:
            ref[place * n : (place + 1) * n, :] = parts[part]


LEFT = (0, 1, 0)
RIGHT = (0, 0, 1)


class Route:
    def __init__(self, nx, ny, half, src, first, out, second, sems, wanted):
        self.nx, self.ny, self.half, self.src = nx, ny, half, src
        self.first, self.out, self.second = first, out, second
        self.send1, self.recv1, self.send2, self.recv2 = sems
        self.wanted = wanted
        me = lax.axis_index("shard")
        self.me = me
        self.core = me % 2
        self.x = (me // 2) % nx
        self.y = me // (2 * nx)
        self.lines = ((0, nx, self.x, ny, self.y), (1, ny, self.y, nx, self.x))

    def device(self, kind, along, across, core):
        if kind == 0:
            return {"shard": (across * self.nx + along) * 2 + core}
        return {"shard": (along * self.nx + across) * 2 + core}

    def piece(self, kind):
        return self.src.at[pl.ds(kind * self.half, self.half), :]

    def copy1(self, kind, src, entry, slot, device):
        return pltpu.make_async_remote_copy(
            src_ref=src,
            dst_ref=self.first[kind].at[entry],
            send_sem=self.send1.at[kind, slot],
            recv_sem=self.recv1.at[kind, entry],
            device_id=device,
            device_id_type=MESH,
        )

    def own(self, kind, step):
        _, size, pos, _, other = self.lines[kind]
        to = (pos + step) % size
        return self.copy1(
            kind, self.piece(kind), pos * 2 + self.core, step, self.device(kind, to, other, self.core)
        )

    def relay(self, kind, step):
        _, size, pos, _, other = self.lines[kind]
        if step == 0:
            src = self.piece(kind)
            entry = pos * 2 + self.core
        else:
            entry = ((pos - step) % size) * 2 + self.core
            src = self.first[kind].at[entry]
        return self.copy1(
            kind, src, entry, size + step, self.device(kind, pos, other, 1 - self.core)
        )

    def start(self):
        for kind in range(2):
            for step in range(1, self.lines[kind][1]):
                self.own(kind, step).start()
        for kind in range(2):
            self.relay(kind, 0).start()

    def keep(self):
        for kind in range(2):
            _, size, pos, _, other = self.lines[kind]
            self.first[kind][pos * 2 + self.core] = self.piece(kind)[...]

    def pass_on(self, kind):
        _, size, pos, _, other = self.lines[kind]
        for step in range(1, size):
            entry = ((pos - step) % size) * 2 + self.core
            self.copy1(kind, self.piece(kind), entry, 0, self.device(kind, pos, other, self.core)).wait_recv()
            self.relay(kind, step).start()

    def copy2(self, kind, step):
        _, size, pos, across, other = self.lines[kind]
        to = (other + step) % across
        return pltpu.make_async_remote_copy(
            src_ref=self.out[kind].at[step],
            dst_ref=self.second[kind].at[other],
            send_sem=self.send2.at[kind, step],
            recv_sem=self.recv2.at[kind, other],
            device_id=self.device(kind, pos, to, self.core),
            device_id_type=MESH,
        )

    def entry_of(self, kind, block):
        if kind == 0:
            return block % (2 * self.nx)
        return (block // (2 * self.nx)) * 2 + block % 2

    def choose(self, kind):
        _, size, pos, across, other = self.lines[kind]
        for step in range(size):
            entry = ((pos - step) % size) * 2 + 1 - self.core
            self.copy1(kind, self.piece(kind), entry, 0, self.device(kind, pos, other, self.core)).wait_recv()
        for step in range(1, across):
            to = (other + step) % across
            block = self.wanted(self.device(kind, pos, to, self.core)["shard"])
            self.out[kind][step] = self.first[kind][self.entry_of(kind, block)]
            self.copy2(kind, step).start()
        block = self.wanted(self.me)
        self.second[kind][other] = self.first[kind][self.entry_of(kind, block)]

    def take(self, kind):
        _, size, pos, across, other = self.lines[kind]
        for step in range(1, across):
            frm = (other - step) % across
            pltpu.make_async_remote_copy(
                src_ref=self.out[kind].at[step],
                dst_ref=self.second[kind].at[frm],
                send_sem=self.send2.at[kind, step],
                recv_sem=self.recv2.at[kind, frm],
                device_id=self.device(kind, pos, (other + step) % across, self.core),
                device_id_type=MESH,
            ).wait_recv()
        block = self.wanted(self.me)
        index = block // (2 * self.nx) if kind == 0 else (block // 2) % self.nx
        return self.second[kind][index]

    def finish(self):
        for kind in range(2):
            _, size, pos, across, other = self.lines[kind]
            for step in range(1, size):
                self.own(kind, step).wait_send()
            for step in range(size):
                self.relay(kind, step).wait_send()
            for step in range(1, across):
                self.copy2(kind, step).wait_send()


def kernel(nx, ny, nz, entries, *refs):
    (grads, table, moment, second, left, right, pbasis, qbasis) = refs[:8]
    (o_up, o_m, o_v, o_l, o_r, o_p, o_q) = refs[8:15]
    (
        g_v, m_v, v_v, l_v, r_v, p_v, q_v,
        gg, up, mrot, y_s, a_s,
        ptl, plh, qr, qnt, qtl, x1, x2, x3,
        fx, fy, gx, gy, sx, sy,
        rfx, rfy, rgx, rgy, rsx, rsy,
        es, ebuf, ezs, ez,
        in_sem, out_sem, s1, r1, s2, r2, t1, u1, t2, u2, esend, erecv, zsend, zrecv,
    ) = refs[15:]
    n = g_v.shape[0]
    half = n // 2
    shards = nx * ny * 2
    me = lax.axis_index("shard")
    mz = lax.axis_index("tensor")

    order = ((grads, g_v), (pbasis, p_v), (left, l_v), (moment, m_v), (qbasis, q_v), (second, v_v), (right, r_v))
    loads = [pltpu.make_async_copy(a, b, in_sem.at[i]) for i, (a, b) in enumerate(order)]
    for load in loads:
        load.start()

    barrier = pltpu.get_barrier_semaphore()
    for step in range(1, shards):
        pl.semaphore_signal(barrier, inc=1, device_id={"shard": (me + step) % shards}, device_id_type=MESH)
    for step in range(1, nz):
        pl.semaphore_signal(barrier, inc=1, device_id={"tensor": (mz + step) % nz}, device_id_type=MESH)

    def row_of_slot(device):
        found = jnp.int32(0)
        for k in range(shards):
            found = jnp.where(table[0, k] == device, k, found)
        return found

    used = jnp.bool_(False)
    for k in range(shards):
        used = used | (table[0, k] == me)

    gather = Route(nx, ny, half, g_v, (fx, fy), (gx, gy), (sx, sy), (s1, r1, s2, r2), row_of_slot)
    give = Route(
        nx, ny, half, up, (rfx, rfy), (rgx, rgy), (rsx, rsy), (t1, u1, t2, u2), lambda d: table[0, d]
    )

    loads[0].wait()
    pl.semaphore_wait(barrier, shards - 1 + nz - 1)
    gather.start()

    gf = g_v[...].astype(F32)
    part = jnp.sum((gf * gf).reshape(n // 8, 8, n), axis=0)
    total = part[:, :128]
    for k in range(1, n // 128):
        total = total + part[:, k * 128 : (k + 1) * 128]
    es[...] = total
    ebuf[me] = total

    def energy_copy(step, src_of):
        return pltpu.make_async_remote_copy(
            src_ref=es,
            dst_ref=ebuf.at[src_of],
            send_sem=esend.at[step],
            recv_sem=erecv.at[src_of],
            device_id={"shard": (me + step) % shards},
            device_id_type=MESH,
        )

    def energy_copy_z(step, src_of):
        return pltpu.make_async_remote_copy(
            src_ref=ezs,
            dst_ref=ez.at[src_of],
            send_sem=zsend.at[step],
            recv_sem=zrecv.at[src_of],
            device_id={"tensor": (mz + step) % nz},
            device_id_type=MESH,
        )

    for step in range(1, shards):
        energy_copy(step, me).start()
    gather.keep()

    stores = []

    def store(src, dst):
        copy = pltpu.make_async_copy(src, dst, out_sem.at[len(stores)])
        copy.start()
        stores.append(copy)

    def orth(basis, out, points):
        y = y_s[...]
        y = y * lax.rsqrt(jnp.sum(y * y) + 1e-12)
        for sweep in range(NS_ITERS):
            y_s[...] = y
            put(x3, y, LEFT, 1)
            put(x2, y, RIGHT, 1)
            put(x1, y, RIGHT, 0)
            a = nt(x3[...], x2[...])
            a_s[...] = a
            points.pop(0)()
            put(x3, a, LEFT, 1)
            put(x2, a, RIGHT, 1)
            b = nt(x3[...], x2[...])
            put(x3, QUINTIC_B * a_s[...] + QUINTIC_C * b, LEFT, 1)
            points.pop(0)()
            y = QUINTIC_A * y_s[...] + nn(x3[...], x1[...])
        basis[...] = jnp.where(used, y.T, basis[...])
        store(basis, out)

    def nothing():
        pass

    loads[1].wait()
    p = p_v[...]
    put(plh, p, LEFT, 1)
    put(ptl, p.T, LEFT, 1)
    loads[2].wait()
    put(x2, l_v[...], RIGHT, 1)
    y_s[...] = nt(ptl[...], x2[...])

    def energy_z():
        for step in range(1, shards):
            energy_copy(step, (me - step) % shards).wait_recv()
        total = jnp.sum(ebuf[...], axis=0)
        ezs[...] = total
        ez[mz] = total
        for step in range(1, nz):
            energy_copy_z(step, mz).start()

    def passing():
        gather.pass_on(0)
        gather.pass_on(1)

    def choosing():
        gather.choose(0)
        gather.choose(1)

    orth(p_v, o_p, [energy_z, nothing, passing, choosing])

    loads[4].wait()
    q = q_v[...]
    put(qr, q, RIGHT, 0)
    put(qnt, q, RIGHT, 1)
    put(qtl, q.T, LEFT, 1)
    loads[3].wait()
    put(x1, m_v[...], RIGHT, 0)
    put(x3, nn(ptl[...], x1[...]), LEFT, 1)
    mrot[...] = nn(x3[...], qr[...])

    for step in range(1, nz):
        energy_copy_z(step, (mz - step) % nz).wait_recv()
    energy = jnp.sum(jnp.sum(ez[...], axis=0), keepdims=True)
    factor = jnp.minimum(1.0, CLIP_RMS / jnp.sqrt(energy / entries + 1e-12))

    gg[0:half, :] = gather.take(0)
    gg[half:n, :] = gather.take(1)
    g = gg[...]
    x1[0:n, :] = g
    x1[n : 2 * n, :] = g
    put(x3, nn(ptl[:, 0 : 2 * n], x1[0 : 2 * n, :]), LEFT, 1)
    rotated = factor * nn(x3[...], qr[...])
    loads[5].wait()
    v_new = BETA_SECOND * v_v[...] + (1.0 - BETA_SECOND) * rotated * rotated
    direction = (BETA_MOMENT * mrot[...] + (1.0 - BETA_MOMENT) * rotated) / (jnp.sqrt(v_new) + ADAM_EPSILON)
    v_v[...] = jnp.where(used, v_new, v_v[...])
    put(x1, direction, RIGHT, 0)
    store(v_v, o_v)
    put(x3, nn(plh[...], x1[...]), LEFT, 1)
    up[...] = nt(x3[...], qnt[...]).astype(BF16)
    give.start()
    give.keep()

    keep_m = jnp.where(used, BETA_MOMENT, 1.0)
    add_m = jnp.where(used, (1.0 - BETA_MOMENT) * factor, 0.0)
    keep_s = jnp.where(used, BETA_STATS, 1.0)
    add_s = jnp.where(used, (1.0 - BETA_STATS) * factor * factor / n, 0.0)
    m_v[...] = keep_m * m_v[...] + add_m * gg[...].astype(F32)
    store(m_v, o_m)
    loads[6].wait()
    put(x2, r_v[...], RIGHT, 1)
    y_s[...] = nt(qtl[...], x2[...])
    g = gg[...]
    l_v[...] = keep_s * l_v[...] + add_s * nt(g, g)
    store(l_v, o_l)
    gt = g.T
    r_v[...] = keep_s * r_v[...] + add_s * nt(gt, gt)
    store(r_v, o_r)

    def giving():
        give.pass_on(0)
        give.pass_on(1)

    def picking():
        give.choose(0)
        give.choose(1)

    orth(q_v, o_q, [nothing, nothing, giving, picking])

    gather.finish()
    for step in range(1, shards):
        energy_copy(step, me).wait_send()
    for step in range(1, nz):
        energy_copy_z(step, mz).wait_send()
    gg[0:half, :] = give.take(0)
    gg[half:n, :] = give.take(1)
    store(gg, o_up)
    give.finish()
    for copy in stores:
        copy.wait()


def shards_program(nx, ny, nz, entries, grads, assignment, *states):
    n = grads.shape[1]
    half = n // 2
    states = [s.reshape(n, n) for s in states]
    square = lambda dtype: pltpu.VMEM((n, n), dtype)
    wide = pltpu.VMEM((n, 3 * n), BF16)
    tall = pltpu.VMEM((3 * n, n), BF16)
    pieces = lambda count: pltpu.VMEM((count, half, n), BF16)
    longest = max(nx, ny)
    dma = lambda *shape: pltpu.SemaphoreType.DMA(shape)
    route = [pieces(2 * nx), pieces(2 * ny), pieces(ny), pieces(nx), pieces(ny), pieces(nx)]
    route_sems = [dma(2, 2 * longest), dma(2, 2 * longest), dma(2, longest), dma(2, longest)]
    shards = nx * ny * 2
    scratch = (
        [square(BF16)] + [square(F32)] * 6
        + [square(BF16), square(BF16), square(F32), square(F32), square(F32)]
        + [wide, wide, tall, wide, wide, tall, wide, wide]
        + route + route
        + [pltpu.VMEM((8, 128), F32), pltpu.VMEM((shards, 8, 128), F32)]
        + [pltpu.VMEM((8, 128), F32), pltpu.VMEM((nz, 8, 128), F32)]
        + [dma(7), dma(7)] + route_sems + route_sems
        + [dma(shards), dma(shards), dma(nz), dma(nz)]
    )
    hbm = pl.BlockSpec(memory_space=pl.ANY)
    out = pl.pallas_call(
        functools.partial(kernel, nx, ny, nz, entries),
        out_shape=[jax.ShapeDtypeStruct((n, n), BF16)] + [jax.ShapeDtypeStruct((n, n), F32)] * 6,
        in_specs=[hbm, pl.BlockSpec(memory_space=pltpu.SMEM)] + [hbm] * 6,
        out_specs=[hbm] * 7,
        scratch_shapes=scratch,
        compiler_params=pltpu.CompilerParams(
            collective_id=0, has_side_effects=True, vmem_limit_bytes=56 * 1024 * 1024
        ),
        cost_estimate=pl.CostEstimate(flops=62 * 2 * n**3, bytes_accessed=52 * n * n, transcendentals=0),
    )(grads, assignment, *states)
    return (out[0],) + tuple(o[None] for o in out[1:])


def solution(mesh):
    shard_count = mesh.shape["shard"]
    chips = shard_count // 2
    nx = 1
    while nx * nx < chips:
        nx *= 2
    ny = chips // nx
    nz = mesh.shape["tensor"]
    state = P("shard", "tensor", None)

    def run(grads, assignment, *states):
        entries = grads.shape[0] * grads.shape[1]
        program = functools.partial(shards_program, nx, ny, nz, entries)
        return jax.shard_map(
            program,
            mesh=mesh,
            in_specs=(P("shard", "tensor"), P("tensor", None)) + (state,) * 6,
            out_specs=(P("shard", "tensor"),) + (state,) * 6,
            check_vma=False,
        )(grads, assignment, *states)

    return run
```

time: 228 us -> 62.5 us (0.27); the launches traced: 224 us -> 62.1 us
  matrix products: 58.7 us -> 0 us
  waiting for transfers between devices: 51.7 us -> 0 us
  Pallas kernels: 0 us -> 50.5 us
  blocking collectives: 42.3 us -> 0 us
  local copies, waits for them, and re-layouts: 42.8 us -> 10.9 us
  between operations: 15.7 us -> 0.66 us
  other arithmetic: 9.63 us -> 0 us
  loops' own time: 2.61 us -> 0 us
    dot_general x22 -> x0, matrix products: 58.7 us -> none  [the longest x20 53.3 us: highest_dot(): jnp.dot(left_side, right_side, precision=lax.Precision.HIGHEST, preferred...]
    reduce_scatter x1 -> x0, waiting for transfers between devices: 51.6 us -> none  [shards(): lax.psum_scatter(partial_value.astype(jnp.bfloat16), 'shard', scatter_dim...]
    pallas_call x0 -> x1, Pallas kernels: none -> 50.5 us  [shards_program(): pl.pallas_call(functools.partial(kernel, nx, ny, nz, entries), out_shape=...]
    psum x1 -> x0, blocking collectives: 42.3 us -> none  [shards(): energy = lax.psum(jnp.sum(grad_float * grad_float), ('shard', 'tensor'))]
    gather x1 -> x0, local copies, waits for them, and re-layouts: 17.4 us -> none  [shards(): jnp.take(updates[slot_index], jnp.clip(tile_row, 0, block_size - 1), axis=0)]
    unnamed x25 -> x19, local copies, waits for them, and re-layouts: 25.3 us -> 10.9 us
    convert_element_type x1 -> x0, other arithmetic: 5.25 us -> none  [shards(): partial_value.astype(jnp.bfloat16)]
    another operation x1 -> x0, loops' own time: 2.61 us -> none  [shards(): lax.cond(in_use[slot_index], lambda values: tile_update(values[0], factor...]
  transfers between devices with their start and end apart: 2 -> 0, of which waited for: 1 -> 0; matrix products, arithmetic and copies ran while one was open for 2% -> 0% of each run, Pallas kernels for 0% -> 0%
where the time goes in v1:
time: 62.5 us; the launch traced here: 62.1 us
  Pallas kernels  50.5 us (81%)
  local copies, waits for them, and re-layouts  10.9 us (17%)
  between operations  0.66 us (1%)
    pallas_call x1, Pallas kernels, shards_program(): pl.pallas_call(functools.partial(kernel, nx, ny, nz, entries), out_shape=...  50.5 us
    unnamed x19, local copies, waits for them, and re-layouts  10.9 us

profile of v1, /device:TPU:0, one launch (start us, length us, event | category | flops | bytes accessed | tf_op | source)
XLA Modules:
  0.0 62.1 jit_solution(16924172515244968799)
XLA Ops:
  0.6 50.5 %shard_map.135 = (bf16[512,512]{1,0:T(8,128)(2,1)}, f32[512,512]{1,0:T(8,128)}, f32[512,512]{1,0:T(8,128)}, f32[512,512]{1,0:T(8,128)}, f32[512,512]{1,0:T(8,128...) custom-call(bf16[512,512]{1,0:T(8,128)(2,1)} %refs_0_.1, s32[1,8]{1,0:T(1,128)} %refs_1_.1, f32[512,512]{1,0:T(8,128)} %bitcast.18, ...), custom_call_target="tpu_custom_call" | custom-call | flops 16642998272 | bytes 13631488 | tf_op jit(solution)/shard_map/pallas_call | solution.py:410
  51.1 0.0 copy-start.5
  51.1 2.0 %copy.22 = bf16[512,512]{1,0:T(8,128)(2,1)} copy(bf16[512,512]{1,0:T(8,128)(2,1)} %get-tuple-element.28) | data formatting | bytes 1048576
  53.1 0.0 copy-done.5
  53.1 0.0 copy-start.4
  53.1 1.0 %copy.23 = f32[1,512,512]{2,1,0:T(8,128)} copy(f32[1,512,512]{2,1,0:T(8,128)S(1)} %bitcast.17) | data formatting | bytes 2097152
  54.1 0.6 %copy-done.4 = f32[512,512]{1,0:T(8,128)S(1)} copy-done((f32[512,512]{1,0:T(8,128)S(1)}, f32[512,512]{1,0:T(8,128)}, u32[]{:S(2)}) %copy-start.4) | copy-done | bytes 1048600
  54.7 0.0 copy-start.3
  54.7 1.0 %copy.24 = f32[1,512,512]{2,1,0:T(8,128)} copy(f32[1,512,512]{2,1,0:T(8,128)S(1)} %bitcast.16) | data formatting | bytes 2097152
  55.7 0.6 %copy-done.3 = f32[512,512]{1,0:T(8,128)S(1)} copy-done((f32[512,512]{1,0:T(8,128)S(1)}, f32[512,512]{1,0:T(8,128)}, u32[]{:S(2)}) %copy-start.3) | copy-done | bytes 1048600
  56.3 0.0 copy-start.2
  56.3 1.0 %copy.25 = f32[1,512,512]{2,1,0:T(8,128)} copy(f32[1,512,512]{2,1,0:T(8,128)S(1)} %bitcast.15) | data formatting | bytes 2097152
  57.3 0.6 %copy-done.2 = f32[512,512]{1,0:T(8,128)S(1)} copy-done((f32[512,512]{1,0:T(8,128)S(1)}, f32[512,512]{1,0:T(8,128)}, u32[]{:S(2)}) %copy-start.2) | copy-done | bytes 1048600
  57.9 0.0 copy-start.1
  57.9 1.0 %copy.26 = f32[1,512,512]{2,1,0:T(8,128)} copy(f32[1,512,512]{2,1,0:T(8,128)S(1)} %bitcast.14) | data formatting | bytes 2097152
  58.9 0.6 %copy-done.1 = f32[512,512]{1,0:T(8,128)S(1)} copy-done((f32[512,512]{1,0:T(8,128)S(1)}, f32[512,512]{1,0:T(8,128)}, u32[]{:S(2)}) %copy-start.1) | copy-done | bytes 1048600
  59.5 0.0 copy-start
  59.5 1.0 %copy.27 = f32[1,512,512]{2,1,0:T(8,128)} copy(f32[1,512,512]{2,1,0:T(8,128)S(1)} %bitcast.13) | data formatting | bytes 2097152
  60.5 0.6 %copy-done = f32[512,512]{1,0:T(8,128)S(1)} copy-done((f32[512,512]{1,0:T(8,128)S(1)}, f32[512,512]{1,0:T(8,128)}, u32[]{:S(2)}) %copy-start) | copy-done | bytes 1048600
  61.1 1.0 %copy.28 = f32[1,512,512]{2,1,0:T(8,128)} copy(f32[1,512,512]{2,1,0:T(8,128)S(1)} %bitcast.12) | data formatting | bytes 2097152
Async XLA Ops:
  51.1 2.0 %copy-start.5 = (f32[512,512]{1,0:T(8,128)S(1)}, f32[512,512]{1,0:T(8,128)}, u32[]{:S(2)}) copy-start(f32[512,512]{1,0:T(8,128)} %get-tuple-element.15) | copy-start | bytes 3145732
  53.1 1.6 %copy-start.4 = (f32[512,512]{1,0:T(8,128)S(1)}, f32[512,512]{1,0:T(8,128)}, u32[]{:S(2)}) copy-start(f32[512,512]{1,0:T(8,128)} %get-tuple-element.16) | copy-start | bytes 3145732
  54.7 1.6 %copy-start.3 = (f32[512,512]{1,0:T(8,128)S(1)}, f32[512,512]{1,0:T(8,128)}, u32[]{:S(2)}) copy-start(f32[512,512]{1,0:T(8,128)} %get-tuple-element.17) | copy-start | bytes 3145732
  56.3 1.6 %copy-start.2 = (f32[512,512]{1,0:T(8,128)S(1)}, f32[512,512]{1,0:T(8,128)}, u32[]{:S(2)}) copy-start(f32[512,512]{1,0:T(8,128)} %get-tuple-element.18) | copy-start | bytes 3145732
  57.9 1.6 %copy-start.1 = (f32[512,512]{1,0:T(8,128)S(1)}, f32[512,512]{1,0:T(8,128)}, u32[]{:S(2)}) copy-start(f32[512,512]{1,0:T(8,128)} %get-tuple-element.19) | copy-start | bytes 3145732
  59.5 1.6 %copy-start = (f32[512,512]{1,0:T(8,128)S(1)}, f32[512,512]{1,0:T(8,128)}, u32[]{:S(2)}) copy-start(f32[512,512]{1,0:T(8,128)} %get-tuple-element.20) | copy-start | bytes 3145732

commit v2 on v1

v2 whole, which is shorter than its diff:
```python
import functools

import jax
import jax.numpy as jnp
from jax import lax
from jax.experimental import pallas as pl
from jax.experimental.pallas import tpu as pltpu
from jax.sharding import PartitionSpec as P

NS_ITERS = 2
PARTS = 2
LIMIT = 48
BETA_MOMENT = 0.9
BETA_SECOND = 0.9
BETA_STATS = 0.9
ADAM_EPSILON = 1e-08
CLIP_RMS = 1.0
QUINTIC_A = 3.4445
QUINTIC_B = -4.775
QUINTIC_C = 2.0315
MESH = pl.DeviceIdType.MESH
F32 = jnp.float32
BF16 = jnp.bfloat16


def nn(a, b):
    return jnp.dot(a, b, preferred_element_type=F32)


def nt(a, b):
    return lax.dot_general(a, b, (((1,), (1,)), ((), ())), preferred_element_type=F32)


def split(x):
    high = x.astype(BF16)
    return high, (x - high.astype(F32)).astype(BF16)


def put(ref, x, order, axis):
    n = x.shape[0]
    parts = split(x)
    for place, part in enumerate(order):
        if axis:
            ref[:, place * n : (place + 1) * n] = parts[part]
        else:
            ref[place * n : (place + 1) * n, :] = parts[part]


LEFT = (0, 1, 0)
RIGHT = (0, 0, 1)


class Route:
    def __init__(self, nx, ny, rows, src, first, out, second, sems, wanted):
        self.nx, self.ny, self.rows, self.src = nx, ny, rows, src
        self.first, self.out, self.second = first, out, second
        self.send1, self.recv1, self.send2, self.recv2 = sems
        self.wanted = wanted
        me = lax.axis_index("shard")
        self.me = me
        self.core = me % 2
        self.x = (me // 2) % nx
        self.y = me // (2 * nx)
        self.lines = ((nx, self.x, ny, self.y), (ny, self.y, nx, self.x))

    def device(self, kind, along, across, core):
        if kind == 0:
            return {"shard": (across * self.nx + along) * 2 + core}
        return {"shard": (along * self.nx + across) * 2 + core}

    def strip(self, part):
        return slice(part * self.rows, (part + 1) * self.rows)

    def piece(self, kind, part):
        return self.src.at[self.strip(part * 2 + kind), :]

    def copy1(self, kind, part, src, entry, slot, device):
        return pltpu.make_async_remote_copy(
            src_ref=src,
            dst_ref=self.first[kind][part].at[entry],
            send_sem=self.send1.at[kind, part, slot],
            recv_sem=self.recv1.at[kind, part, entry],
            device_id=device,
            device_id_type=MESH,
        )

    def own(self, kind, part, step):
        size, pos, _, other = self.lines[kind]
        device = self.device(kind, (pos + step) % size, other, self.core)
        return self.copy1(kind, part, self.piece(kind, part), pos * 2 + self.core, step, device)

    def relay(self, kind, part, step):
        size, pos, _, other = self.lines[kind]
        entry = ((pos + size - step) % size) * 2 + self.core
        src = self.first[kind][part].at[entry] if step else self.piece(kind, part)
        device = self.device(kind, pos, other, 1 - self.core)
        return self.copy1(kind, part, src, entry, size + step, device)

    def start(self, part):
        for kind in range(2):
            for step in range(1, self.lines[kind][0]):
                self.own(kind, part, step).start()
        for kind in range(2):
            self.relay(kind, part, 0).start()
        for kind in range(2):
            _, pos, _, _ = self.lines[kind]
            self.first[kind][part][pos * 2 + self.core] = self.piece(kind, part)[...]

    def arrived(self, kind, part, entry):
        _, pos, _, other = self.lines[kind]
        device = self.device(kind, pos, other, 1 - self.core)
        self.copy1(kind, part, self.piece(kind, part), entry, 0, device).wait_recv()

    def pass_on(self, part):
        for kind in range(2):
            size, pos, _, _ = self.lines[kind]
            for step in range(1, size):
                self.arrived(kind, part, ((pos + size - step) % size) * 2 + self.core)
                self.relay(kind, part, step).start()

    def copy2(self, kind, part, step, place):
        _, pos, across, other = self.lines[kind]
        return pltpu.make_async_remote_copy(
            src_ref=self.out[kind][part].at[step],
            dst_ref=self.second[kind][part].at[place],
            send_sem=self.send2.at[kind, part, step],
            recv_sem=self.recv2.at[kind, part, place],
            device_id=self.device(kind, pos, (other + step) % across, self.core),
            device_id_type=MESH,
        )

    def entry_of(self, kind, block):
        if kind == 0:
            return block % (2 * self.nx)
        return (block // (2 * self.nx)) * 2 + block % 2

    def choose(self, part):
        for kind in range(2):
            size, pos, across, other = self.lines[kind]
            for step in range(size):
                self.arrived(kind, part, ((pos + size - step) % size) * 2 + 1 - self.core)
            for step in range(1, across):
                to = (other + step) % across
                block = self.wanted(self.device(kind, pos, to, self.core)["shard"])
                self.out[kind][part][step] = self.first[kind][part][self.entry_of(kind, block)]
                self.copy2(kind, part, step, other).start()
            entry = self.entry_of(kind, self.wanted(self.me))
            self.second[kind][part][other] = self.first[kind][part][entry]

    def take(self, part, ref):
        block = self.wanted(self.me)
        for kind in range(2):
            _, _, across, other = self.lines[kind]
            for step in range(1, across):
                self.copy2(kind, part, step, (other + across - step) % across).wait_recv()
            index = block // (2 * self.nx) if kind == 0 else (block // 2) % self.nx
            ref[self.strip(part * 2 + kind), :] = self.second[kind][part][index]

    def finish(self):
        for kind in range(2):
            size, _, across, other = self.lines[kind]
            for part in range(PARTS):
                for step in range(1, size):
                    self.own(kind, part, step).wait_send()
                for step in range(size):
                    self.relay(kind, part, step).wait_send()
                for step in range(1, across):
                    self.copy2(kind, part, step, other).wait_send()


def kernel(nx, ny, nz, entries, *refs):
    (grads, table, moment, second, left, right, pbasis, qbasis) = refs[:8]
    (o_up, o_m, o_v, o_l, o_r, o_p, o_q) = refs[8:15]
    (
        g_v, m_v, v_v, l_v, r_v, p_v, q_v,
        gg, up, mrot, y_s, a_s,
        ptl, plh, qr, qnt, qtl, x1, x2, x3,
        es, ebuf, ezs, ez,
        in_sem, s1, r1, s2, r2, t1, u1, t2, u2, esend, erecv, zsend, zrecv,
    ) = refs[15 : len(refs) - 12 * PARTS]
    buffers = [refs[len(refs) - PARTS * (12 - i) :][:PARTS] for i in range(12)]
    (fx, fy, gx, gy, sx, sy, rfx, rfy, rgx, rgy, rsx, rsy) = buffers
    n = g_v.shape[0]
    half = n // PARTS
    rows = half // 2
    shards = nx * ny * 2
    me = lax.axis_index("shard")
    mz = lax.axis_index("tensor")

    order = ((grads, g_v), (pbasis, p_v), (left, l_v), (moment, m_v), (qbasis, q_v), (second, v_v), (right, r_v))
    loads = [pltpu.make_async_copy(a, b, in_sem.at[i]) for i, (a, b) in enumerate(order)]
    for load in loads:
        load.start()

    barrier = pltpu.get_barrier_semaphore()
    for step in range(1, shards):
        pl.semaphore_signal(barrier, inc=1, device_id={"shard": (me + step) % shards}, device_id_type=MESH)
    for step in range(1, nz):
        pl.semaphore_signal(barrier, inc=1, device_id={"tensor": (mz + step) % nz}, device_id_type=MESH)

    def row_of_slot(device):
        found = jnp.int32(0)
        for k in range(shards):
            found = jnp.where(table[0, k] == device, k, found)
        return found

    used = jnp.bool_(False)
    for k in range(shards):
        used = used | (table[0, k] == me)

    gather = Route(nx, ny, rows, g_v, (fx, fy), (gx, gy), (sx, sy), (s1, r1, s2, r2), row_of_slot)
    give = Route(
        nx, ny, rows, up, (rfx, rfy), (rgx, rgy), (rsx, rsy), (t1, u1, t2, u2), lambda d: table[0, d]
    )

    loads[0].wait()
    pl.semaphore_wait(barrier, shards - 1 + nz - 1)
    for part in range(PARTS):
        gather.start(part)

    gf = g_v[...].astype(F32)
    part = jnp.sum((gf * gf).reshape(n // 8, 8, n), axis=0)
    total = part[:, :128]
    for k in range(1, n // 128):
        total = total + part[:, k * 128 : (k + 1) * 128]
    es[...] = total
    ebuf[me] = total

    def energy_copy(step, src_of):
        return pltpu.make_async_remote_copy(
            src_ref=es,
            dst_ref=ebuf.at[src_of],
            send_sem=esend.at[step],
            recv_sem=erecv.at[src_of],
            device_id={"shard": (me + step) % shards},
            device_id_type=MESH,
        )

    def energy_copy_z(step, src_of):
        return pltpu.make_async_remote_copy(
            src_ref=ezs,
            dst_ref=ez.at[src_of],
            send_sem=zsend.at[step],
            recv_sem=zrecv.at[src_of],
            device_id={"tensor": (mz + step) % nz},
            device_id_type=MESH,
        )

    for step in range(1, shards):
        energy_copy(step, me).start()

    def orth(basis, out, points):
        points[0]()
        y = y_s[...]
        y = y * lax.rsqrt(jnp.sum(y * y) + 1e-12)
        for sweep in range(NS_ITERS):
            y_s[...] = y
            put(x3, y, LEFT, 1)
            put(x2, y, RIGHT, 1)
            put(x1, y, RIGHT, 0)
            points[1 + 3 * sweep]()
            a = nt(x3[...], x2[...])
            a_s[...] = a
            put(x3, a, LEFT, 1)
            put(x2, a, RIGHT, 1)
            points[2 + 3 * sweep]()
            b = nt(x3[...], x2[...])
            put(x3, QUINTIC_B * a_s[...] + QUINTIC_C * b, LEFT, 1)
            points[3 + 3 * sweep]()
            y = QUINTIC_A * y_s[...] + nn(x3[...], x1[...])
        out[...] = jnp.where(used, y.T, basis[...])

    def nothing():
        pass

    loads[1].wait()
    p = p_v[...]
    put(plh, p, LEFT, 1)
    put(ptl, p.T, LEFT, 1)
    loads[2].wait()
    put(x2, l_v[...], RIGHT, 1)
    y_s[...] = nt(ptl[...], x2[...])

    def energy_z():
        for step in range(1, shards):
            energy_copy(step, (me - step) % shards).wait_recv()
        total = jnp.sum(ebuf[...], axis=0)
        ezs[...] = total
        ez[mz] = total
        for step in range(1, nz):
            energy_copy_z(step, mz).start()

    def act(route, name, part):
        return lambda: getattr(route, name)(part)

    orth(
        p_v,
        o_p,
        [
            nothing,
            act(gather, "pass_on", 0),
            act(gather, "choose", 0),
            act(gather, "pass_on", 1),
            act(gather, "choose", 1),
            energy_z,
            nothing,
        ],
    )

    loads[4].wait()
    q = q_v[...]
    put(qr, q, RIGHT, 0)
    put(qnt, q, RIGHT, 1)
    put(qtl, q.T, LEFT, 1)
    loads[3].wait()
    put(x1, m_v[...], RIGHT, 0)
    put(x3, nn(ptl[...], x1[...]), LEFT, 1)
    mrot[...] = nn(x3[...], qr[...])

    for step in range(1, nz):
        energy_copy_z(step, (mz - step) % nz).wait_recv()
    energy = jnp.sum(jnp.sum(ez[...], axis=0), keepdims=True)
    factor = jnp.minimum(1.0, CLIP_RMS / jnp.sqrt(energy / entries + 1e-12))

    for part in range(PARTS):
        gather.take(part, gg)
        g = gg[part * half : (part + 1) * half, :]
        high = nn(ptl[:, part * half : (part + 1) * half], g)
        term = high + nn(ptl[:, n + part * half : n + (part + 1) * half], g)
        a_s[...] = term if part == 0 else a_s[...] + term
    put(x3, a_s[...], LEFT, 1)
    rotated = factor * nn(x3[...], qr[...])
    loads[5].wait()
    v_new = BETA_SECOND * v_v[...] + (1.0 - BETA_SECOND) * rotated * rotated
    direction = (BETA_MOMENT * mrot[...] + (1.0 - BETA_MOMENT) * rotated) / (jnp.sqrt(v_new) + ADAM_EPSILON)
    o_v[...] = jnp.where(used, v_new, v_v[...])
    put(x1, direction, RIGHT, 0)
    for part in range(PARTS):
        strip = slice(part * half, (part + 1) * half)
        high, low = split(nn(plh[strip, :], x1[...]))
        x3[strip, 0:n] = high
        x3[strip, n : 2 * n] = low
        x3[strip, 2 * n : 3 * n] = high
        up[strip, :] = nt(x3[strip, :], qnt[...]).astype(BF16)
        give.start(part)

    keep_m = jnp.where(used, BETA_MOMENT, 1.0)
    add_m = jnp.where(used, (1.0 - BETA_MOMENT) * factor, 0.0)
    keep_s = jnp.where(used, BETA_STATS, 1.0)
    add_s = jnp.where(used, (1.0 - BETA_STATS) * factor * factor / n, 0.0)
    o_m[...] = keep_m * m_v[...] + add_m * gg[...].astype(F32)
    loads[6].wait()
    put(x2, r_v[...], RIGHT, 1)
    y_s[...] = nt(qtl[...], x2[...])
    g = gg[...]
    o_l[...] = keep_s * l_v[...] + add_s * nt(g, g)
    gt = g.T
    o_r[...] = keep_s * r_v[...] + add_s * nt(gt, gt)

    orth(
        q_v,
        o_q,
        [
            act(give, "pass_on", 0),
            act(give, "choose", 0),
            act(give, "pass_on", 1),
            act(give, "choose", 1),
            nothing,
            nothing,
            nothing,
        ],
    )

    gather.finish()
    for step in range(1, shards):
        energy_copy(step, me).wait_send()
    for step in range(1, nz):
        energy_copy_z(step, mz).wait_send()
    for part in range(PARTS):
        give.take(part, o_up)
    give.finish()


def hand_on(*refs):
    sems = refs[14]
    copies = [pltpu.make_async_copy(refs[i], refs[7 + i], sems.at[i]) for i in range(7)]
    for copy in copies:
        copy.start()
    for copy in copies:
        copy.wait()


def shards_program(nx, ny, nz, entries, grads, assignment, *states):
    n = grads.shape[1]
    half = n // 2
    states = [s.reshape(n, n) for s in states]
    square = lambda dtype: pltpu.VMEM((n, n), dtype)
    wide = pltpu.VMEM((n, 3 * n), BF16)
    tall = pltpu.VMEM((3 * n, n), BF16)
    pieces = lambda count: [pltpu.VMEM((count, half // PARTS, n), BF16)] * PARTS
    longest = max(nx, ny)
    dma = lambda *shape: pltpu.SemaphoreType.DMA(shape)
    route = sum((pieces(count) for count in (2 * nx, 2 * ny, ny, nx, ny, nx)), [])
    route_sems = [dma(2, PARTS, 2 * longest)] * 2 + [dma(2, PARTS, longest)] * 2
    shards = nx * ny * 2
    scratch = (
        [square(BF16)] + [square(F32)] * 6
        + [square(BF16), square(BF16), square(F32), square(F32), square(F32)]
        + [wide, wide, tall, wide, wide, tall, wide, wide]
        + [pltpu.VMEM((8, 128), F32), pltpu.VMEM((shards, 8, 128), F32)]
        + [pltpu.VMEM((8, 128), F32), pltpu.VMEM((nz, 8, 128), F32)]
        + [dma(7)] + route_sems + route_sems
        + [dma(shards), dma(shards), dma(nz), dma(nz)]
        + route + route
    )
    vmem = pl.BlockSpec(memory_space=pltpu.VMEM)
    hbm = pl.BlockSpec(memory_space=pl.ANY)
    out = pl.pallas_call(
        functools.partial(kernel, nx, ny, nz, entries),
        out_shape=[square(BF16)] + [square(F32)] * 6,
        in_specs=[hbm, pl.BlockSpec(memory_space=pltpu.SMEM)] + [hbm] * 6,
        out_specs=[vmem] * 7,
        scratch_shapes=scratch,
        compiler_params=pltpu.CompilerParams(
            collective_id=0, has_side_effects=True, vmem_limit_bytes=LIMIT * 1024 * 1024
        ),
        cost_estimate=pl.CostEstimate(flops=62 * 2 * n**3, bytes_accessed=52 * n * n, transcendentals=0),
    )(grads, assignment, *states)
    out = pl.pallas_call(
        hand_on,
        out_shape=[jax.ShapeDtypeStruct(o.shape, o.dtype) for o in out],
        in_specs=[hbm] * 7,
        out_specs=[hbm] * 7,
        scratch_shapes=[dma(7)],
        compiler_params=pltpu.CompilerParams(vmem_limit_bytes=1024 * 1024),
        cost_estimate=pl.CostEstimate(flops=0, bytes_accessed=52 * n * n, transcendentals=0),
    )(*out)
    return (out[0],) + tuple(o[None] for o in out[1:])


def solution(mesh):
    shard_count = mesh.shape["shard"]
    chips = shard_count // 2
    nx = 1
    while nx * nx < chips:
        nx *= 2
    ny = chips // nx
    nz = mesh.shape["tensor"]
    state = P("shard", "tensor", None)

    def run(grads, assignment, *states):
        entries = grads.shape[0] * grads.shape[1]
        program = functools.partial(shards_program, nx, ny, nz, entries)
        return jax.shard_map(
            program,
            mesh=mesh,
            in_specs=(P("shard", "tensor"), P("tensor", None)) + (state,) * 6,
            out_specs=(P("shard", "tensor"),) + (state,) * 6,
            check_vma=False,
        )(grads, assignment, *states)

    return run
```

time: 62.5 us -> 49.1 us (0.79)
  local copies, waits for them, and re-layouts: 10.9 us -> 0 us
  Pallas kernels: 50.5 us -> 48.2 us
    unnamed x19 -> x0, local copies, waits for them, and re-layouts: 10.9 us -> none
    pallas_call x1, Pallas kernels: 50.5 us -> 45.3 us  [shards_program(): pl.pallas_call(functools.partial(kernel, nx, ny, nz, entries), out_shape=...]
    pallas_call x0 -> x1, Pallas kernels: none -> 2.9 us  [shards_program(): pl.pallas_call(hand_on, out_shape=[jax.ShapeDtypeStruct(o.shape, o.dtype)...]
where the time goes in v2:
time: 49.1 us; the launch traced here: 49 us
  Pallas kernels  48.2 us (98%)
  between operations  0.8 us (2%)
    pallas_call x1, Pallas kernels, shards_program(): pl.pallas_call(functools.partial(kernel, nx, ny, nz, entries), out_shape=...  45.3 us
    pallas_call x1, Pallas kernels, shards_program(): pl.pallas_call(hand_on, out_shape=[jax.ShapeDtypeStruct(o.shape, o.dtype)...  2.9 us

profile of v2, /device:TPU:0, one launch (start us, length us, event | category | flops | bytes accessed | tf_op | source)
XLA Modules:
  0.0 49.0 jit_solution(14238447637341717287)
XLA Ops:
  0.6 45.3 %shard_map.135 = (bf16[512,512]{1,0:T(8,128)(2,1)S(1)}, f32[512,512]{1,0:T(8,128)S(1)}, f32[512,512]{1,0:T(8,128)S(1)}, f32[512,512]{1,0:T(8,128)S(1)}, f32[512,...) custom-call(bf16[512,512]{1,0:T(8,128)(2,1)} %refs_0_.1, s32[1,8]{1,0:T(1,128)} %refs_1_.1, ...), custom_call_target="tpu_custom_call" | custom-call | flops 16642998272 | bytes 13631488 | tf_op jit(solution)/shard_map/pallas_call | solution.py:418
  45.9 2.9 %shard_map.136 = (bf16[512,512]{1,0:T(8,128)(2,1)}, f32[512,512]{1,0:T(8,128)}, f32[512,512]{1,0:T(8,128)}, f32[512,512]{1,0:T(8,128)}, f32[512,512]{1,0:T(8,128...) custom-call(bf16[512,512]{1,0:T(8,128)(2,1)S(1)} %get-tuple-element.21.refs_0_, f32[512,512]{1,0:T(8,128)S(1)} %get-tuple-element.22.refs_1_, ...), custom_call_target="tpu_custom_call" | custom-call | bytes 13631488 | tf_op jit(solution)/shard_map/pallas_call | solution.py:429
